TPU v7x, 32 devices: a whole 2x2x4 slice. The times are simulated.
32 devices in a mesh: section: 4 (over z), ctx: 8 (over y, x, core).
Axes of the slice: x: 2, y: 2, z: 4, core: 2. Of those that a mesh axis runs over, the one named last changes fastest.
Arguments:
- queries: bfloat16 [4, 2048, 2560], P('section', 'ctx'), may hold values from -5 to 5
- keys: bfloat16 [4, 2048, 512], P('section', 'ctx'), may hold values from -5 to 5
- values: bfloat16 [4, 2048, 512], P('section', 'ctx'), may hold values from -6 to 6
- output_cotangent: bfloat16 [4, 2048, 2560], P('section', 'ctx'), may hold values from -6 to 6
- doc_start: int32 [4, 2048], P('section', 'ctx'), may hold values from 0 to 2047, as said below
Outputs:
- attn: bfloat16 [4, 2048, 2560], P('section', 'ctx')
- handed_dq: bfloat16 [4, 2048, 2560], P('section', 'ctx')
- handed_kv: bfloat16 [4, 2, 2048, 512], P('section', None, 'ctx')
Inputs may be any that keep to these rules, and one draw needn't show every extreme that they name: doc_start[m, i] is the first position of the document holding token i; documents are 768 tokens long at most, every microbatch holds one of exactly 768 tokens, and its last token is a document of its own.
All inputs are finite; a program needn't handle non-finite values.
Results may differ from a plain program's by a relative error of at most 0.012.
The roundings to bfloat16 on the way count: a program that leaves them out, or rounds other values in their place, can miss the bound.
Values may be sent and summed in bfloat16 or wider, within the bound.
A program may use at most 64 MiB of HBM per device.

v0:
```python
import jax
import jax.numpy as jnp
from jax import lax
from jax.sharding import PartitionSpec as P

HEAD_WIDTH = 128
REACH = 3


def shifted(value, axis, steps):
    count = lax.axis_size(axis)
    first, last = (max(0, -steps), min(count, count - steps))
    return lax.ppermute(value, axis, [(source, source + steps) for source in range(first, last)])


def group_terms(query_part, dout_part, key_part, value_part, visible, scale):
    scores = (
        jnp.einsum("tgd,wd->gtw", query_part, key_part, preferred_element_type=jnp.float32) * scale
    )
    scores = jnp.where(visible[None], scores, -jnp.inf)
    top = jnp.max(scores, axis=-1, keepdims=True)
    total = jnp.sum(jnp.exp(scores - top), axis=-1, keepdims=True)
    lse = top + jnp.log(total)
    prob = jnp.exp(scores - lse)
    prob_b = prob.astype(jnp.bfloat16)
    attn = jnp.einsum("gtw,wd->tgd", prob_b, value_part, preferred_element_type=jnp.float32).astype(
        jnp.bfloat16
    )
    delta = jnp.sum(dout_part.astype(jnp.float32) * attn.astype(jnp.float32), axis=-1)
    dprob = jnp.einsum("tgd,wd->gtw", dout_part, value_part, preferred_element_type=jnp.float32)
    dscore = (prob * (dprob - jnp.transpose(delta)[:, :, None]) * scale).astype(jnp.bfloat16)
    grad_q = jnp.einsum("gtw,wd->tgd", dscore, key_part, preferred_element_type=jnp.float32).astype(
        jnp.bfloat16
    )
    key_gradient = jnp.einsum("gtw,tgd->wd", dscore, query_part, preferred_element_type=jnp.float32)
    value_gradient = jnp.einsum(
        "gtw,tgd->wd", prob_b, dout_part, preferred_element_type=jnp.float32
    )
    return (attn, grad_q, key_gradient, value_gradient)


def local(queries, keys, values, output_cotangent, doc_start):
    local_tokens = queries.shape[1]
    heads_kv = keys.shape[2] // HEAD_WIDTH
    group_size = queries.shape[2] // keys.shape[2]
    scale = HEAD_WIDTH ** (-0.5)
    token_span = (REACH + 1) * local_tokens
    position = lax.axis_index("ctx")
    leading_entry = position * local_tokens
    query_pos = leading_entry + jnp.arange(local_tokens, dtype=jnp.int32)
    key_pos = leading_entry - REACH * local_tokens + jnp.arange(token_span, dtype=jnp.int32)
    starts = doc_start[0]
    visible = (key_pos[None, :] >= starts[:, None]) & (key_pos[None, :] <= query_pos[:, None])
    own_block = jnp.stack([keys[0], values[0]])
    earlier = []
    moving = own_block
    for stride in range(REACH):
        moving = shifted(moving, "ctx", 1)
        earlier.append(moving)
    attention_window = jnp.concatenate(earlier[::-1] + [own_block], axis=1)
    query_groups = jnp.moveaxis(
        queries[0].reshape(local_tokens, heads_kv, group_size, HEAD_WIDTH), 1, 0
    )
    dout_groups = jnp.moveaxis(
        output_cotangent[0].reshape(local_tokens, heads_kv, group_size, HEAD_WIDTH), 1, 0
    )
    window_groups = jnp.moveaxis(
        attention_window.reshape(2, token_span, heads_kv, HEAD_WIDTH), 2, 1
    )

    def per_group(items):
        return group_terms(items[0], items[1], items[2], items[3], visible, scale)

    attn, grad_q, key_gradient, value_gradient = lax.map(
        per_group, (query_groups, dout_groups, window_groups[0], window_groups[1])
    )
    attn_rows = jnp.moveaxis(attn, 0, 1).reshape(local_tokens, -1)
    grad_q_rows = jnp.moveaxis(grad_q, 0, 1).reshape(local_tokens, -1)
    partial_terms = jnp.stack(
        [
            jnp.moveaxis(key_gradient, 0, 1).reshape(token_span, -1),
            jnp.moveaxis(value_gradient, 0, 1).reshape(token_span, -1),
        ]
    )

    def owner_piece(behind):
        offset = (REACH - behind) * local_tokens
        return partial_terms[:, offset : offset + local_tokens]

    summed = owner_piece(REACH)
    for stride in range(REACH):
        summed = shifted(summed, "ctx", -1) + owner_piece(REACH - 1 - stride)
    kv_grads = summed.astype(jnp.bfloat16)
    handed_dq, handed_kv = shifted((grad_q_rows[None], kv_grads[None]), "section", -1)
    return (attn_rows[None], handed_dq, handed_kv)


def solution(mesh):
    return jax.shard_map(
        local,
        mesh=mesh,
        in_specs=(
            P("section", "ctx", None),
            P("section", "ctx", None),
            P("section", "ctx", None),
            P("section", "ctx", None),
            P("section", "ctx"),
        ),
        out_specs=(
            P("section", "ctx", None),
            P("section", "ctx", None),
            P("section", None, "ctx", None),
        ),
        check_vma=False,
    )
```

profile of v0, /device:TPU:19, one launch (start us, length us, event | category | flops | bytes accessed | tf_op | source)
XLA Modules:
  0.0 184.0 jit_solution(17789034238756937650)
XLA Ops:
  0.6 1.2 copy.25
  1.8 1.1 copy.26
  3.0 3.7 %collective-permute-start = (bf16[2,256,512]{1,2,0:T(8,128)(2,1)S(1)}, bf16[2,256,512]{1,2,0:T(8,128)(2,1)S(1)}, u32[]{:S(2)}, u32[]{:S(2)}) collective-permute-start(bf16[2,256,512]{1,2,0:T(8,128)(2,1)S(1)} %pad_maximum_fusion), channel_id=1, source_target_pairs={{0,1},{1,2},{2,3},{3,4},{4,5},{5,6},{6,7},{8,9},{9,10},{10,11},{11... | collective-permute-start | bytes 1572872 | tf_op jit(solution)/shard_map/ppermute | solution.py:13
  6.7 6.1 %collective-permute-done = bf16[2,256,512]{1,2,0:T(8,128)(2,1)S(1)} collective-permute-done((bf16[2,256,512]{1,2,0:T(8,128)(2,1)S(1)}, bf16[2,256,512]{1,2,0:T(8,128)(2,1)S(1)}, u32[]{:S(2)}, u32[]{:S(2)}) %collective-permute-start) | collective-permute-done | bytes 524320 | tf_op jit(solution)/shard_map/ppermute | solution.py:13
  12.8 0.8 copy-done.5
  13.6 5.3 %collective-permute-start.1 = (bf16[2,256,512]{1,2,0:T(8,128)(2,1)S(1)}, bf16[2,256,512]{1,2,0:T(8,128)(2,1)}, u32[]{:S(2)}, u32[]{:S(2)}) collective-permute-start(bf16[2,256,512]{1,2,0:T(8,128)(2,1)S(1)} %collective-permute-done), channel_id=1, source_target_pairs={{0,1},{1,2},{2,3},{3,4},{4,5},{5,6},{6,7},{8,9},{9,10},{10,11},{11... | collective-permute-start | bytes 1572872 | tf_op jit(solution)/shard_map/ppermute | solution.py:13
  18.9 6.1 %collective-permute-done.1 = bf16[2,256,512]{1,2,0:T(8,128)(2,1)} collective-permute-done((bf16[2,256,512]{1,2,0:T(8,128)(2,1)S(1)}, bf16[2,256,512]{1,2,0:T(8,128)(2,1)}, u32[]{:S(2)}, u32[]{:S(2)}) %collective-permute-start.1) | collective-permute-done | bytes 524320 | tf_op jit(solution)/shard_map/ppermute | solution.py:13
  25.0 5.4 %collective-permute-start.2 = (bf16[2,256,512]{1,2,0:T(8,128)(2,1)}, bf16[2,256,512]{1,2,0:T(8,128)(2,1)}, u32[]{:S(2)}, u32[]{:S(2)}) collective-permute-start(bf16[2,256,512]{1,2,0:T(8,128)(2,1)} %collective-permute-done.1), channel_id=1, source_target_pairs={{0,1},{1,2},{2,3},{3,4},{4,5},{5,6},{6,7},{8,9},{9,10},{10,11},{11... | collective-permute-start | bytes 1572872 | tf_op jit(solution)/shard_map/ppermute | solution.py:13
  30.4 0.6 copy.28
  31.0 2.5 %copy.29 = bf16[1,256,2560]{1,2,0:T(8,128)(2,1)} copy(bf16[1,256,2560]{2,1,0:T(8,128)(2,1)} %param.10) | data formatting | bytes 2621440 | tf_op args[3]
  33.5 3.2 %collective-permute-done.2 = bf16[2,256,512]{1,2,0:T(8,128)(2,1)} collective-permute-done((bf16[2,256,512]{1,2,0:T(8,128)(2,1)}, bf16[2,256,512]{1,2,0:T(8,128)(2,1)}, u32[]{:S(2)}, u32[]{:S(2)}) %collective-permute-start.2) | collective-permute-done | bytes 524320 | tf_op jit(solution)/shard_map/ppermute | solution.py:13
  36.8 1.3 maximum_maximum_fusion
  38.3 0.5 copy-done.7
  38.8 47.1 %while.17 = (s32[]{:T(128)}, bf16[4,256,5,128]{1,3,2,0:T(8,128)(2,1)}, bf16[4,256,5,128]{1,3,2,0:T(8,128)(2,1)}, f32[4,1024,128]{2,1,0:T(8,128)}, f32[4,1024,128...) while((s32[]{:T(128)}, ...), condition=%wide.region_4.5_spmd.clone, body=%wide.region_0.4_spmd.clone.sunk | while | flops 2043868672 | bytes 46021788 | solution.py:74
  38.8 0.3 compare_and_fusion.2
  39.1 1.0 fusion.61
  40.1 1.1 exponential_reduce_fusion.2
  41.4 2.1 %fusion.65 = f32[4,1024,128]{2,1,0:T(8,128)} fusion(f32[4,1024,128]{2,1,0:T(8,128)} %get-tuple-element.234, s32[]{:T(128)} %get-tuple-element.230, bf16[4,256,5,128]{1,3,2,0:T(8,128)(2,1)S(1)} %copy-done.1, f32[1024,256,5]{1,0,2:T(8,128)S(1)} %get-tuple-element.213, f32[5,256]{1,0:T(8,128)S(1)} %log_add_fusion.2, ...), kind=kOutput, calls=%fused_computation.11.clone.1 | convolution fusion | flops 340787200 | bytes 6366208 | tf_op jit(solution)/shard_map/while/body/eval_jaxpr/gtw,tgd->wd/dot_general | solution.py:36
  43.5 2.2 %bitcast_dynamic-update-slice_fusion.2 = (bf16[4,256,5,128]{1,3,2,0:T(8,128)(2,1)}, bf16[128,5,256]{2,0,1:T(8,128)(2,1)S(1)}) fusion(bf16[4,256,5,128]{1,3,2,0:T(8,128)(2,1)} %get-tuple-element.231, s32[]{:T(128)} %get-tuple-element.230, f32[1024,256,5]{1,0,2:T(8,128)S(1)} %get-tuple-element.213, f32[5,256]{1,0:T(8,128)S(1)} %log_add_fusion.2, ...), kind=kOutput, calls=%fused_computation.23.clone.1 | convolution fusion | flops 340951040 | bytes 6431744 | tf_op jit(solution)/shard_map/while/body/eval_jaxpr/gtw,wd->tgd/dot_general | solution.py:26
  45.9 1.8 fusion.62
  47.7 1.6 fusion.64
  49.3 1.3 fusion.63
  50.8 1.0 fusion.61
  51.9 1.1 exponential_reduce_fusion.2
  53.2 2.1 %fusion.65 = f32[4,1024,128]{2,1,0:T(8,128)} fusion(f32[4,1024,128]{2,1,0:T(8,128)} %get-tuple-element.234, s32[]{:T(128)} %get-tuple-element.230, bf16[4,256,5,128]{1,3,2,0:T(8,128)(2,1)S(1)} %copy-done.1, f32[1024,256,5]{1,0,2:T(8,128)S(1)} %get-tuple-element.213, f32[5,256]{1,0:T(8,128)S(1)} %log_add_fusion.2, ...), kind=kOutput, calls=%fused_computation.11.clone.1 | convolution fusion | flops 340787200 | bytes 6366208 | tf_op jit(solution)/shard_map/while/body/eval_jaxpr/gtw,tgd->wd/dot_general | solution.py:36
  55.3 2.2 %bitcast_dynamic-update-slice_fusion.2 = (bf16[4,256,5,128]{1,3,2,0:T(8,128)(2,1)}, bf16[128,5,256]{2,0,1:T(8,128)(2,1)S(1)}) fusion(bf16[4,256,5,128]{1,3,2,0:T(8,128)(2,1)} %get-tuple-element.231, s32[]{:T(128)} %get-tuple-element.230, f32[1024,256,5]{1,0,2:T(8,128)S(1)} %get-tuple-element.213, f32[5,256]{1,0:T(8,128)S(1)} %log_add_fusion.2, ...), kind=kOutput, calls=%fused_computation.23.clone.1 | convolution fusion | flops 340951040 | bytes 6431744 | tf_op jit(solution)/shard_map/while/body/eval_jaxpr/gtw,wd->tgd/dot_general | solution.py:26
  57.6 1.8 fusion.62
  59.4 1.6 fusion.64
  61.1 1.3 fusion.63
  62.6 1.0 fusion.61
  63.7 1.1 exponential_reduce_fusion.2
  65.0 2.2 %fusion.65 = f32[4,1024,128]{2,1,0:T(8,128)} fusion(f32[4,1024,128]{2,1,0:T(8,128)} %get-tuple-element.234, s32[]{:T(128)} %get-tuple-element.230, bf16[4,256,5,128]{1,3,2,0:T(8,128)(2,1)S(1)} %copy-done.1, f32[1024,256,5]{1,0,2:T(8,128)S(1)} %get-tuple-element.213, f32[5,256]{1,0:T(8,128)S(1)} %log_add_fusion.2, ...), kind=kOutput, calls=%fused_computation.11.clone.1 | convolution fusion | flops 340787200 | bytes 6366208 | tf_op jit(solution)/shard_map/while/body/eval_jaxpr/gtw,tgd->wd/dot_general | solution.py:36
  67.1 2.2 %bitcast_dynamic-update-slice_fusion.2 = (bf16[4,256,5,128]{1,3,2,0:T(8,128)(2,1)}, bf16[128,5,256]{2,0,1:T(8,128)(2,1)S(1)}) fusion(bf16[4,256,5,128]{1,3,2,0:T(8,128)(2,1)} %get-tuple-element.231, s32[]{:T(128)} %get-tuple-element.230, f32[1024,256,5]{1,0,2:T(8,128)S(1)} %get-tuple-element.213, f32[5,256]{1,0:T(8,128)S(1)} %log_add_fusion.2, ...), kind=kOutput, calls=%fused_computation.23.clone.1 | convolution fusion | flops 340951040 | bytes 6431744 | tf_op jit(solution)/shard_map/while/body/eval_jaxpr/gtw,wd->tgd/dot_general | solution.py:26
  69.4 1.8 fusion.62
  71.2 1.7 fusion.64
  72.9 1.3 fusion.63
  74.5 1.0 fusion.61
  75.5 1.1 exponential_reduce_fusion.2
  76.8 2.1 %fusion.65 = f32[4,1024,128]{2,1,0:T(8,128)} fusion(f32[4,1024,128]{2,1,0:T(8,128)} %get-tuple-element.234, s32[]{:T(128)} %get-tuple-element.230, bf16[4,256,5,128]{1,3,2,0:T(8,128)(2,1)S(1)} %copy-done.1, f32[1024,256,5]{1,0,2:T(8,128)S(1)} %get-tuple-element.213, f32[5,256]{1,0:T(8,128)S(1)} %log_add_fusion.2, ...), kind=kOutput, calls=%fused_computation.11.clone.1 | convolution fusion | flops 340787200 | bytes 6366208 | tf_op jit(solution)/shard_map/while/body/eval_jaxpr/gtw,tgd->wd/dot_general | solution.py:36
  78.9 2.2 %bitcast_dynamic-update-slice_fusion.2 = (bf16[4,256,5,128]{1,3,2,0:T(8,128)(2,1)}, bf16[128,5,256]{2,0,1:T(8,128)(2,1)S(1)}) fusion(bf16[4,256,5,128]{1,3,2,0:T(8,128)(2,1)} %get-tuple-element.231, s32[]{:T(128)} %get-tuple-element.230, f32[1024,256,5]{1,0,2:T(8,128)S(1)} %get-tuple-element.213, f32[5,256]{1,0:T(8,128)S(1)} %log_add_fusion.2, ...), kind=kOutput, calls=%fused_computation.23.clone.1 | convolution fusion | flops 340951040 | bytes 6431744 | tf_op jit(solution)/shard_map/while/body/eval_jaxpr/gtw,wd->tgd/dot_general | solution.py:26
  81.2 1.8 fusion.62
  83.1 1.6 fusion.64
  84.7 1.2 fusion.63
  85.9 2.9 %copy.33 = f32[1024,4,128]{2,1,0:T(4,128)S(1)} copy(f32[1024,4,128]{2,0,1:T(8,128)} %bitcast.156) | data formatting | bytes 4194304 | tf_op jit(solution)/shard_map/transpose | solution.py:81
  88.9 1.9 %stack_reshape.6 = f32[1,1024,512]{2,1,0:T(8,128)} reshape(f32[1024,4,128]{2,1,0:T(4,128)S(1)} %copy.33) | data formatting | bytes 4194304 | tf_op jit(solution)/shard_map/stack;reshape | solution.py:79
  90.8 3.2 %constant_dynamic-update-slice_fusion.1 = f32[2,1024,512]{2,1,0:T(8,128)} fusion(f32[1,1024,512]{2,1,0:T(8,128)} %stack_reshape.6), kind=kLoop, calls=%fused_computation.55 | loop fusion | bytes 4194304
  94.0 2.7 %copy.34 = f32[1024,4,128]{2,1,0:T(4,128)} copy(f32[1024,4,128]{2,0,1:T(8,128)S(1)} %bitcast.157) | data formatting | bytes 4194304 | tf_op jit(solution)/shard_map/transpose | solution.py:82
  96.7 2.1 %stack_reshape.7 = f32[1,1024,512]{2,1,0:T(8,128)S(1)} reshape(f32[1024,4,128]{2,1,0:T(4,128)} %copy.34) | data formatting | bytes 4194304 | tf_op jit(solution)/shard_map/stack;reshape | solution.py:79
  98.8 1.5 constant_dynamic-update-slice_fusion
  100.3 1.4 slice.26
  101.7 2.1 %collective-permute-start.4 = (f32[2,256,512]{2,1,0:T(8,128)S(1)}, f32[2,256,512]{2,1,0:T(8,128)S(1)}, u32[]{:S(2)}, u32[]{:S(2)}) collective-permute-start(f32[2,256,512]{2,1,0:T(8,128)S(1)} %slice.26), channel_id=1, source_target_pairs={{1,0},{2,1},{3,2},{4,3},{5,4},{6,5},{7,6},{9,8},{10,9},{11,10},{12... | collective-permute-start | bytes 3145736 | tf_op jit(solution)/shard_map/ppermute | solution.py:13
  103.8 15.8 %collective-permute-done.4 = f32[2,256,512]{2,1,0:T(8,128)S(1)} collective-permute-done((f32[2,256,512]{2,1,0:T(8,128)S(1)}, f32[2,256,512]{2,1,0:T(8,128)S(1)}, u32[]{:S(2)}, u32[]{:S(2)}) %collective-permute-start.4) | collective-permute-done | bytes 1048608 | tf_op jit(solution)/shard_map/ppermute | solution.py:13
  119.6 1.4 slice_add_fusion.2
  121.1 2.1 %collective-permute-start.5 = (f32[2,256,512]{2,1,0:T(8,128)S(1)}, f32[2,256,512]{2,1,0:T(8,128)S(1)}, u32[]{:S(2)}, u32[]{:S(2)}) collective-permute-start(f32[2,256,512]{2,1,0:T(8,128)S(1)} %slice_add_fusion.2), channel_id=1, source_target_pairs={{1,0},{2,1},{3,2},{4,3},{5,4},{6,5},{7,6},{9,8},{10,9},{11,10},{12... | collective-permute-start | bytes 3145736 | tf_op jit(solution)/shard_map/ppermute | solution.py:13
  123.1 15.1 %collective-permute-done.5 = f32[2,256,512]{2,1,0:T(8,128)S(1)} collective-permute-done((f32[2,256,512]{2,1,0:T(8,128)S(1)}, f32[2,256,512]{2,1,0:T(8,128)S(1)}, u32[]{:S(2)}, u32[]{:S(2)}) %collective-permute-start.5) | collective-permute-done | bytes 1048608 | tf_op jit(solution)/shard_map/ppermute | solution.py:13
  138.4 1.9 %collective-permute-start.6 = (f32[2,256,512]{2,1,0:T(8,128)S(1)}, f32[2,256,512]{2,1,0:T(8,128)S(1)}, u32[]{:S(2)}, u32[]{:S(2)}) collective-permute-start(f32[2,256,512]{2,1,0:T(8,128)S(1)} %slice_add_fusion.1), channel_id=1, source_target_pairs={{1,0},{2,1},{3,2},{4,3},{5,4},{6,5},{7,6},{9,8},{10,9},{11,10},{12... | collective-permute-start | bytes 3145736 | tf_op jit(solution)/shard_map/ppermute | solution.py:13
  140.4 2.1 %collective-permute-start.3 = (bf16[1,256,2560]{1,2,0:T(8,128)(2,1)}, bf16[1,256,2560]{1,2,0:T(8,128)(2,1)S(1)}, u32[]{:S(2)}, u32[]{:S(2)}) collective-permute-start(bf16[1,256,2560]{1,2,0:T(8,128)(2,1)} %bitcast.13), channel_id=1, source_target_pairs={{8,0},{16,8},{24,16},{9,1},{17,9},{25,17},{10,2},{18,10},{26,18},{... | collective-permute-start | bytes 3932168 | tf_op jit(solution)/shard_map/ppermute | solution.py:13
  142.4 13.0 %collective-permute-done.6 = f32[2,256,512]{2,1,0:T(8,128)S(1)} collective-permute-done((f32[2,256,512]{2,1,0:T(8,128)S(1)}, f32[2,256,512]{2,1,0:T(8,128)S(1)}, u32[]{:S(2)}, u32[]{:S(2)}) %collective-permute-start.6) | collective-permute-done | bytes 1048608 | tf_op jit(solution)/shard_map/ppermute | solution.py:13
  155.7 2.1 %collective-permute-start.7 = (bf16[1,2,256,512]{3,2,1,0:T(8,128)(2,1)S(1)}, bf16[1,2,256,512]{3,2,1,0:T(8,128)(2,1)}, u32[]{:S(2)}, u32[]{:S(2)}) collective-permute-start(bf16[1,2,256,512]{3,2,1,0:T(8,128)(2,1)S(1)} %fusion.37), channel_id=1, source_target_pairs={{8,0},{16,8},{24,16},{9,1},{17,9},{25,17},{10,2},{18,10},{26,18},{... | collective-permute-start | bytes 1572872 | tf_op jit(solution)/shard_map/ppermute | solution.py:13
  157.8 1.6 copy.35
  159.4 14.0 %collective-permute-done.3 = bf16[1,256,2560]{1,2,0:T(8,128)(2,1)S(1)} collective-permute-done((bf16[1,256,2560]{1,2,0:T(8,128)(2,1)}, bf16[1,256,2560]{1,2,0:T(8,128)(2,1)S(1)}, u32[]{:S(2)}, u32[]{:S(2)}) %collective-permute-start.3) | collective-permute-done | bytes 1310752 | tf_op jit(solution)/shard_map/ppermute | solution.py:13
  173.4 1.6 copy.36
  175.0 7.1 %collective-permute-done.7 = bf16[1,2,256,512]{3,2,1,0:T(8,128)(2,1)} collective-permute-done((bf16[1,2,256,512]{3,2,1,0:T(8,128)(2,1)S(1)}, bf16[1,2,256,512]{3,2,1,0:T(8,128)(2,1)}, u32[]{:S(2)}, u32[]{:S(2)}) %collective-permute-start.7) | collective-permute-done | bytes 524320 | tf_op jit(solution)/shard_map/ppermute | solution.py:13
  182.1 1.9 %copy.71 = bf16[1,2,256,512]{3,2,1,0:T(8,128)(2,1)} copy(bf16[1,2,256,512]{3,2,1,0:T(8,128)(2,1)} %collective-permute-done.7) | data formatting | bytes 1048576
  (41 shorter events, 2.8 us)
Async XLA Ops:
  0.6 29.8 %copy-start.3 = (bf16[1,256,2560]{2,1,0:T(8,128)(2,1)S(1)}, bf16[1,256,2560]{2,1,0:T(8,128)(2,1)}, u32[]{:S(2)}) copy-start(bf16[1,256,2560]{2,1,0:T(8,128)(2,1)} %param.7) | copy-start | bytes 3932164
  3.0 9.8 %collective-permute-start = (bf16[2,256,512]{1,2,0:T(8,128)(2,1)S(1)}, bf16[2,256,512]{1,2,0:T(8,128)(2,1)S(1)}, u32[]{:S(2)}, u32[]{:S(2)}) collective-permute-start(bf16[2,256,512]{1,2,0:T(8,128)(2,1)S(1)} %pad_maximum_fusion), channel_id=1, source_target_pairs={{0,1},{1,2},{2,3},{3,4},{4,5},{5,6},{6,7},{8,9},{9,10},{10,11},{11... | collective-permute-start | bytes 1572872 | tf_op jit(solution)/shard_map/ppermute | solution.py:13
  12.8 0.8 copy-start.5
  13.6 11.4 %collective-permute-start.1 = (bf16[2,256,512]{1,2,0:T(8,128)(2,1)S(1)}, bf16[2,256,512]{1,2,0:T(8,128)(2,1)}, u32[]{:S(2)}, u32[]{:S(2)}) collective-permute-start(bf16[2,256,512]{1,2,0:T(8,128)(2,1)S(1)} %collective-permute-done), channel_id=1, source_target_pairs={{0,1},{1,2},{2,3},{3,4},{4,5},{5,6},{6,7},{8,9},{9,10},{10,11},{11... | collective-permute-start | bytes 1572872 | tf_op jit(solution)/shard_map/ppermute | solution.py:13
  25.0 11.8 %collective-permute-start.2 = (bf16[2,256,512]{1,2,0:T(8,128)(2,1)}, bf16[2,256,512]{1,2,0:T(8,128)(2,1)}, u32[]{:S(2)}, u32[]{:S(2)}) collective-permute-start(bf16[2,256,512]{1,2,0:T(8,128)(2,1)} %collective-permute-done.1), channel_id=1, source_target_pairs={{0,1},{1,2},{2,3},{3,4},{4,5},{5,6},{6,7},{8,9},{9,10},{10,11},{11... | collective-permute-start | bytes 1572872 | tf_op jit(solution)/shard_map/ppermute | solution.py:13
  31.0 5.8 %copy-start.6 = (bf16[2,256,512]{1,2,0:T(8,128)(2,1)S(1)}, bf16[2,256,512]{1,2,0:T(8,128)(2,1)}, u32[]{:S(2)}) copy-start(bf16[2,256,512]{1,2,0:T(8,128)(2,1)} %copy-done.5) | copy-start | bytes 1572868
  38.1 0.7 copy-start.7
  40.1 1.3 copy-start.1
  51.9 1.3 copy-start.1
  63.6 1.3 copy-start.1
  75.5 1.3 copy-start.1
  90.8 3.2 %copy-start.2 = (f32[4,1024,128]{2,1,0:T(8,128)S(1)}, f32[4,1024,128]{2,1,0:T(8,128)}, u32[]{:S(2)}) copy-start(f32[4,1024,128]{2,1,0:T(8,128)} %get-tuple-element.61) | copy-start | bytes 6291460
  100.3 37.9 %copy-start = (f32[2,1024,512]{2,1,0:T(8,128)S(1)}, f32[2,1024,512]{2,1,0:T(8,128)}, u32[]{:S(2)}) copy-start(f32[2,1024,512]{2,1,0:T(8,128)} %constant_dynamic-update-slice_fusion) | copy-start | bytes 12582916
  101.7 17.9 %collective-permute-start.4 = (f32[2,256,512]{2,1,0:T(8,128)S(1)}, f32[2,256,512]{2,1,0:T(8,128)S(1)}, u32[]{:S(2)}, u32[]{:S(2)}) collective-permute-start(f32[2,256,512]{2,1,0:T(8,128)S(1)} %slice.26), channel_id=1, source_target_pairs={{1,0},{2,1},{3,2},{4,3},{5,4},{6,5},{7,6},{9,8},{10,9},{11,10},{12... | collective-permute-start | bytes 3145736 | tf_op jit(solution)/shard_map/ppermute | solution.py:13
  121.1 36.7 %copy-start.4 = (bf16[4,256,5,128]{1,3,2,0:T(8,128)(2,1)S(1)}, bf16[4,256,5,128]{1,3,2,0:T(8,128)(2,1)}, u32[]{:S(2)}) copy-start(bf16[4,256,5,128]{1,3,2,0:T(8,128)(2,1)} %get-tuple-element.58) | copy-start | bytes 3932164
  121.1 17.1 %collective-permute-start.5 = (f32[2,256,512]{2,1,0:T(8,128)S(1)}, f32[2,256,512]{2,1,0:T(8,128)S(1)}, u32[]{:S(2)}, u32[]{:S(2)}) collective-permute-start(f32[2,256,512]{2,1,0:T(8,128)S(1)} %slice_add_fusion.2), channel_id=1, source_target_pairs={{1,0},{2,1},{3,2},{4,3},{5,4},{6,5},{7,6},{9,8},{10,9},{11,10},{12... | collective-permute-start | bytes 3145736 | tf_op jit(solution)/shard_map/ppermute | solution.py:13
  138.4 17.0 %collective-permute-start.6 = (f32[2,256,512]{2,1,0:T(8,128)S(1)}, f32[2,256,512]{2,1,0:T(8,128)S(1)}, u32[]{:S(2)}, u32[]{:S(2)}) collective-permute-start(f32[2,256,512]{2,1,0:T(8,128)S(1)} %slice_add_fusion.1), channel_id=1, source_target_pairs={{1,0},{2,1},{3,2},{4,3},{5,4},{6,5},{7,6},{9,8},{10,9},{11,10},{12... | collective-permute-start | bytes 3145736 | tf_op jit(solution)/shard_map/ppermute | solution.py:13
  140.4 33.1 %collective-permute-start.3 = (bf16[1,256,2560]{1,2,0:T(8,128)(2,1)}, bf16[1,256,2560]{1,2,0:T(8,128)(2,1)S(1)}, u32[]{:S(2)}, u32[]{:S(2)}) collective-permute-start(bf16[1,256,2560]{1,2,0:T(8,128)(2,1)} %bitcast.13), channel_id=1, source_target_pairs={{8,0},{16,8},{24,16},{9,1},{17,9},{25,17},{10,2},{18,10},{26,18},{... | collective-permute-start | bytes 3932168 | tf_op jit(solution)/shard_map/ppermute | solution.py:13
  155.7 26.4 %collective-permute-start.7 = (bf16[1,2,256,512]{3,2,1,0:T(8,128)(2,1)S(1)}, bf16[1,2,256,512]{3,2,1,0:T(8,128)(2,1)}, u32[]{:S(2)}, u32[]{:S(2)}) collective-permute-start(bf16[1,2,256,512]{3,2,1,0:T(8,128)(2,1)S(1)} %fusion.37), channel_id=1, source_target_pairs={{8,0},{16,8},{24,16},{9,1},{17,9},{25,17},{10,2},{18,10},{26,18},{... | collective-permute-start | bytes 1572872 | tf_op jit(solution)/shard_map/ppermute | solution.py:13
where the time goes:
time: 186 us; the launch traced here: 184 us
  waiting for transfers between devices  80.5 us (43%)
  matrix products  40.2 us (22%)
  local copies, waits for them, and re-layouts  28.4 us (15%)
  starting transfers between devices  24.5 us (13%)
  other arithmetic  9.2 us (5%)
    ppermute x8, waiting for transfers between devices, shifted(): lax.ppermute(value, axis, [(source, source + steps) for source in range(f...  80.5 us
    ppermute x8, starting transfers between devices, shifted(): lax.ppermute(value, axis, [(source, source + steps) for source in range(f...  24.5 us
    unnamed x22, local copies, waits for them, and re-layouts  14.9 us
    dot_general x4, matrix products, group_terms(): jnp.einsum('gtw,wd->tgd', prob_b, value_part, preferred_element_type=jnp....  8.8 us
    dot_general x4, matrix products, group_terms(): jnp.einsum('gtw,tgd->wd', prob_b, dout_part, preferred_element_type=jnp.f...  8.5 us
    dot_general x4, matrix products, group_terms(): jnp.einsum('tgd,wd->gtw', dout_part, value_part, preferred_element_type=j...  7.25 us
    dot_general x4, matrix products, group_terms(): jnp.einsum('gtw,tgd->wd', dscore, query_part, preferred_element_type=jnp....  6.58 us
    another operation x3, local copies, waits for them, and re-layouts, local(): jnp.stack([jnp.moveaxis(key_gradient, 0, 1).reshape(token_span, -1), jnp....  5.47 us
  transfers between devices with their start and end apart: 8, of which 8 were waited for; matrix products, arithmetic and copies ran while one was open for 4% of the time, Pallas kernels for 0%

commit v1 on v0

v1 whole, which is shorter than its diff:
```python
import functools

import jax
import jax.numpy as jnp
from jax import lax
from jax.experimental import pallas as pl
from jax.experimental.pallas import tpu as pltpu
from jax.sharding import PartitionSpec as P

WIDTH = 128
REACH = 3
LOG2E = 1.4426950408889634
HIDDEN = -1e30
MESH = pl.DeviceIdType.MESH
NT = (((1,), (1,)), ((), ()))
NN = (((1,), (0,)), ((), ()))
TN = (((0,), (0,)), ((), ()))


def dot(a, b, dims):
    return lax.dot_general(a, b, dims, preferred_element_type=jnp.float32)


def body(
    n, sections, groups, per,
    doc_ref, q_hbm, k_hbm, v_hbm, do_hbm,
    attn_hbm, dq_hbm, kv_hbm,
    win, q_v, do_v, attn_v, dq_v, bias, acc, own, part, xbuf, xin, rbuf, rin, zbuf,
    kvl_sem, ql_sem, al_sem, kv_send, kv_recv, x_send, x_recv, r_send, r_recv,
    dq_send, dq_recv, z_send, z_recv,
):
    tok = q_v.shape[0]
    sec, d = lax.axis_index("section"), lax.axis_index("ctx")
    odd = lax.rem(d, 2) == 1
    even = lax.rem(d, 2) == 0
    mate = d + 1 - 2 * lax.rem(d, 2)
    has = {-1: d >= 1, -3: d >= 3, 1: d + 1 < n, 3: d + 3 < n}
    up, down = sec + 1 < sections, sec >= 1
    scale = WIDTH ** (-0.5)

    def slot(s):
        return pl.ds(s * tok, tok)

    def lanes(i, count=1):
        return pl.ds(pl.multiple_of(i * count * WIDTH, WIDTH), count * WIDTH)

    def load_kv(g, which):
        src = (k_hbm, v_hbm)[which]
        return pltpu.make_async_copy(
            src.at[:, lanes(g)], win.at[g, which, slot(REACH), :], kvl_sem.at[g, which]
        )

    def load_q(g, which):
        src, dst = ((q_hbm, q_v), (do_hbm, do_v))[which]
        return pltpu.make_async_copy(
            src.at[:, lanes(g, per)], dst.at[:, lanes(g, per)], ql_sem.at[g, which]
        )

    def store_attn(g):
        return pltpu.make_async_copy(
            attn_v.at[:, lanes(g, per)], attn_hbm.at[:, lanes(g, per)], al_sem.at[g]
        )

    def kv_copy(g, src_slot, dst_slot, kind, target):
        return pltpu.make_async_remote_copy(
            src_ref=win.at[g, :, slot(src_slot), :],
            dst_ref=win.at[g, :, slot(dst_slot), :],
            send_sem=kv_send.at[g, kind],
            recv_sem=kv_recv.at[g, dst_slot],
            device_id=(sec, target),
            device_id_type=MESH,
        )

    def x_copy(g):
        return pltpu.make_async_remote_copy(
            src_ref=xbuf.at[g], dst_ref=xin.at[g], send_sem=x_send.at[g], recv_sem=x_recv.at[g],
            device_id=(sec, mate), device_id_type=MESH,
        )

    def r_copy(g, i):
        return pltpu.make_async_remote_copy(
            src_ref=rbuf.at[g, i], dst_ref=rin.at[g, i],
            send_sem=r_send.at[g, i], recv_sem=r_recv.at[g, i],
            device_id=(sec, d - (1, 3)[i]), device_id_type=MESH,
        )

    def dq_copy(h):
        return pltpu.make_async_remote_copy(
            src_ref=dq_v.at[h], dst_ref=dq_hbm.at[:, lanes(h)],
            send_sem=dq_send.at[h], recv_sem=dq_recv.at[h],
            device_id=(sec - 1, d), device_id_type=MESH,
        )

    def z_copy(g):
        return pltpu.make_async_remote_copy(
            src_ref=zbuf.at[g], dst_ref=kv_hbm.at[:, :, lanes(g)],
            send_sem=z_send.at[g], recv_sem=z_recv.at[g],
            device_id=(sec - 1, d), device_id_type=MESH,
        )

    def send_own(g):
        load_kv(g, 0).wait()
        load_kv(g, 1).wait()
        pl.when(has[1])(lambda: kv_copy(g, 3, 2, 0, d + 1).start())
        pl.when(has[3])(lambda: kv_copy(g, 3, 0, 1, d + 3).start())

    def forward(g):
        @pl.when(has[-1] & even)
        def _():
            kv_copy(g, 2, 2, 0, d).wait_recv()
            kv_copy(g, 2, 1, 2, mate).start()

        @pl.when(has[-3] & odd)
        def _():
            kv_copy(g, 0, 0, 1, d).wait_recv()
            kv_copy(g, 0, 1, 2, mate).start()

    def arrive(g):
        pl.when(has[-1] & odd)(lambda: kv_copy(g, 2, 2, 0, d).wait_recv())
        pl.when(has[-3] & even)(lambda: kv_copy(g, 0, 0, 1, d).wait_recv())
        pl.when(d >= 2)(lambda: kv_copy(g, 1, 1, 2, d).wait_recv())

    def give(g):
        own[g] = acc[:, slot(3), :]
        part[g, 0] = acc[:, slot(2), :]
        part[g, 1] = acc[:, slot(0), :]
        xbuf[g] = acc[:, slot(1), :].astype(jnp.bfloat16)
        pl.when(d >= 2)(lambda: x_copy(g).start())

    def pass_on(g):
        @pl.when(d >= 2)
        def _():
            x_copy(g).wait_recv()

            @pl.when(even)
            def _():
                part[g, 0] += xin[g].astype(jnp.float32)

            @pl.when(odd)
            def _():
                part[g, 1] += xin[g].astype(jnp.float32)

        @pl.when(has[-1])
        def _():
            rbuf[g, 0] = part[g, 0].astype(jnp.bfloat16)
            r_copy(g, 0).start()

        @pl.when(has[-3])
        def _():
            rbuf[g, 1] = part[g, 1].astype(jnp.bfloat16)
            r_copy(g, 1).start()

    def finish(g):
        @pl.when(has[1])
        def _():
            r_copy(g, 0).wait_recv()
            own[g] += rin[g, 0].astype(jnp.float32)

        @pl.when(has[3])
        def _():
            r_copy(g, 1).wait_recv()
            own[g] += rin[g, 1].astype(jnp.float32)

        zbuf[g] = own[g].astype(jnp.bfloat16)
        pl.when(down)(lambda: z_copy(g).start())

    for g in range(groups):
        load_kv(g, 0).start()
        load_kv(g, 1).start()
        if g == 0:
            load_q(0, 0).start()
            load_q(0, 1).start()
    for g in range(1, groups):
        load_q(g, 0).start()
        load_q(g, 1).start()

    barrier = pltpu.get_barrier_semaphore()

    def greet(there, where):
        @pl.when(there)
        def _():
            pl.semaphore_signal(barrier, inc=1, device_id=where, device_id_type=MESH)

    for off in (-1, 1, -3, 3):
        greet(has[off], (sec, d + off))
    greet(up, (sec + 1, d))
    greet(down, (sec - 1, d))
    peers = sum(x.astype(jnp.int32) for x in (has[-1], has[1], has[-3], has[3], up, down))
    pl.semaphore_wait(barrier, peers)

    send_own(0)

    for s, missing in ((2, d < 1), (1, d < 2), (0, d < 3)):
        @pl.when(missing)
        def _():
            for g in range(groups):
                win[g, :, slot(s), :] = jnp.zeros((2, tok, WIDTH), win.dtype)

    starts = jnp.transpose(jnp.broadcast_to(doc_ref[...], (tok, tok)))
    rows = d * tok + lax.broadcasted_iota(jnp.int32, (tok, tok), 0)
    columns = lax.broadcasted_iota(jnp.int32, (tok, tok), 1)
    for s in range(REACH + 1):
        key_pos = (d - REACH + s) * tok + columns
        seen = (key_pos >= starts) & (key_pos <= rows)
        bias[:, slot(s)] = jnp.where(seen, 0.0, HIDDEN)

    forward(0)

    def head(g, i):
        h = g * per + i
        q, do = q_v[:, lanes(h)], do_v[:, lanes(h)]
        keys, values = win[g, 0], win[g, 1]
        t = dot(q, keys, NT) * (scale * LOG2E) + bias[...]
        top = jnp.max(t, axis=1, keepdims=True)
        p = jnp.exp2(t - top)
        prob = p * (1.0 / jnp.sum(p, axis=1, keepdims=True))
        prob_b = prob.astype(jnp.bfloat16)
        attn = dot(prob_b, values, NN).astype(jnp.bfloat16)
        attn_v[:, lanes(h)] = attn
        delta = jnp.sum(do.astype(jnp.float32) * attn.astype(jnp.float32), axis=1, keepdims=True)
        dprob = dot(do, values, NT)
        ds = (prob * (dprob - delta) * scale).astype(jnp.bfloat16)
        dq_v[h] = dot(ds, keys, NN).astype(jnp.bfloat16)
        pl.when(down)(lambda: dq_copy(h).start())
        gk, gv = dot(ds, q, TN), dot(prob_b, do, TN)
        if i == 0:
            acc[0], acc[1] = gk, gv
        else:
            acc[0] += gk
            acc[1] += gv

    def group(g, _):
        load_q(g, 0).wait()
        load_q(g, 1).wait()
        arrive(g)
        pl.when(g + 1 < groups)(lambda: send_own(g + 1))
        for i in range(per):
            head(g, i)
            if i == 1:
                pl.when(g >= 1)(lambda: pass_on(g - 1))
            if i == 3:
                pl.when(g + 1 < groups)(lambda: forward(g + 1))
        store_attn(g).start()
        give(g)
        pl.when(g >= 1)(lambda: finish(g - 1))
        return 0

    lax.fori_loop(0, groups, group, 0)
    pass_on(groups - 1)
    finish(groups - 1)

    def drain(g, _):
        store_attn(g).wait()
        pl.when(has[1])(lambda: kv_copy(g, 3, 2, 0, d + 1).wait_send())
        pl.when(has[3])(lambda: kv_copy(g, 3, 0, 1, d + 3).wait_send())
        pl.when((has[-1] & even) | (has[-3] & odd))(lambda: kv_copy(g, 2, 1, 2, mate).wait_send())
        pl.when(d >= 2)(lambda: x_copy(g).wait_send())
        pl.when(has[-1])(lambda: r_copy(g, 0).wait_send())
        pl.when(has[-3])(lambda: r_copy(g, 1).wait_send())

        def each(i, _):
            pl.when(down)(lambda: dq_copy(g * per + i).wait_send())
            pl.when(up)(lambda: dq_copy(g * per + i).wait_recv())
            return 0

        lax.fori_loop(0, per, each, 0)
        pl.when(down)(lambda: z_copy(g).wait_send())
        pl.when(up)(lambda: z_copy(g).wait_recv())
        return 0

    lax.fori_loop(0, groups, drain, 0)


def solution(mesh):
    n, sections = mesh.shape["ctx"], mesh.shape["section"]

    def local(queries, keys, values, output_cotangent, doc_start):
        tok, wide = queries.shape[1:]
        narrow = keys.shape[2]
        groups, per = narrow // WIDTH, wide // narrow
        heads = groups * per
        bf, f4 = jnp.bfloat16, jnp.float32
        dma = pltpu.SemaphoreType.DMA
        anywhere = pl.BlockSpec(memory_space=pl.ANY)
        attn, dq, kv = pl.pallas_call(
            functools.partial(body, n, sections, groups, per),
            out_shape=(
                jax.ShapeDtypeStruct((tok, wide), bf),
                jax.ShapeDtypeStruct((tok, wide), bf),
                jax.ShapeDtypeStruct((2, tok, narrow), bf),
            ),
            in_specs=[pl.BlockSpec(memory_space=pltpu.VMEM)] + [anywhere] * 4,
            out_specs=(anywhere,) * 3,
            scratch_shapes=[
                pltpu.VMEM((groups, 2, (REACH + 1) * tok, WIDTH), bf),
                pltpu.VMEM((tok, wide), bf),
                pltpu.VMEM((tok, wide), bf),
                pltpu.VMEM((tok, wide), bf),
                pltpu.VMEM((heads, tok, WIDTH), bf),
                pltpu.VMEM((tok, (REACH + 1) * tok), f4),
                pltpu.VMEM((2, (REACH + 1) * tok, WIDTH), f4),
                pltpu.VMEM((groups, 2, tok, WIDTH), f4),
                pltpu.VMEM((groups, 2, 2, tok, WIDTH), f4),
                pltpu.VMEM((groups, 2, tok, WIDTH), bf),
                pltpu.VMEM((groups, 2, tok, WIDTH), bf),
                pltpu.VMEM((groups, 2, 2, tok, WIDTH), bf),
                pltpu.VMEM((groups, 2, 2, tok, WIDTH), bf),
                pltpu.VMEM((groups, 2, tok, WIDTH), bf),
                dma((groups, 2)), dma((groups, 2)), dma((groups,)),
                dma((groups, 3)), dma((groups, 3)),
                dma((groups,)), dma((groups,)),
                dma((groups, 2)), dma((groups, 2)),
                dma((heads,)), dma((heads,)),
                dma((groups,)), dma((groups,)),
            ],
            compiler_params=pltpu.CompilerParams(
                collective_id=0, has_side_effects=True, vmem_limit_bytes=48 * 2**20
            ),
        )(doc_start, queries[0], keys[0], values[0], output_cotangent[0])
        last = lax.axis_index("section") == sections - 1
        dq = jnp.where(last, jnp.zeros_like(dq), dq)
        kv = jnp.where(last, jnp.zeros_like(kv), kv)
        return attn[None], dq[None], kv[None]

    rows = P("section", "ctx", None)
    return jax.shard_map(
        local,
        mesh=mesh,
        in_specs=(rows, rows, rows, rows, P("section", "ctx")),
        out_specs=(rows, rows, P("section", None, "ctx", None)),
        check_vma=False,
    )
```

time: 186 us -> 61.5 us (0.33)
  waiting for transfers between devices: 80.5 us -> 0 us
  Pallas kernels: 0 us -> 53.7 us
  matrix products: 40.2 us -> 0 us
  starting transfers between devices: 24.5 us -> 0 us
  local copies, waits for them, and re-layouts: 28.4 us -> 4.94 us
  other arithmetic: 9.2 us -> 1.98 us
    ppermute x8 -> x0, waiting for transfers between devices: 80.5 us -> none  [shifted(): lax.ppermute(value, axis, [(source, source + steps) for source in range(f...]
    pallas_call x0 -> x1, Pallas kernels: none -> 53.7 us  [local(): pl.pallas_call(functools.partial(body, n, sections, groups, per), out_sha...]
    dot_general x24 -> x0, matrix products: 40.2 us -> none  [the longest x4 8.8 us: group_terms(): jnp.einsum('gtw,wd->tgd', prob_b, value_part, preferred_element_type=jnp....]
    ppermute x8 -> x0, starting transfers between devices: 24.5 us -> none  [shifted(): lax.ppermute(value, axis, [(source, source + steps) for source in range(f...]
    unnamed x22 -> x9, local copies, waits for them, and re-layouts: 14.9 us -> 4.94 us
    transpose x2 -> x0, local copies, waits for them, and re-layouts: 5.62 us -> none  [the longest x1 2.94 us: local(): jnp.moveaxis(key_gradient, 0, 1).reshape(token_span, -1)]
    another operation x3 -> x0, local copies, waits for them, and re-layouts: 5.47 us -> none  [local(): jnp.stack([jnp.moveaxis(key_gradient, 0, 1).reshape(token_span, -1), jnp....]
    reduce_sum x8 -> x0, other arithmetic: 4.8 us -> none  [the longest x4 4.38 us: group_terms(): total = jnp.sum(jnp.exp(scores - top), axis=-1, keepdims=True)]
  transfers between devices with their start and end apart: 8 -> 0, of which waited for: 8 -> 0; matrix products, arithmetic and copies ran while one was open for 4% -> 0% of each run, Pallas kernels for 0% -> 0%
where the time goes in v1:
time: 61.5 us; the launch traced here: 61.3 us
  Pallas kernels  53.7 us (87%)
  local copies, waits for them, and re-layouts  4.94 us (8%)
  other arithmetic  1.98 us (3%)
  between operations  0.66 us (1%)
    pallas_call x1, Pallas kernels, local(): pl.pallas_call(functools.partial(body, n, sections, groups, per), out_sha...  53.7 us
    unnamed x9, local copies, waits for them, and re-layouts  4.94 us
    broadcast_in_dim x2, other arithmetic, local(): return (attn[None], dq[None], kv[None])  1.98 us

profile of v1, /device:TPU:19, one launch (start us, length us, event | category | flops | bytes accessed | tf_op | source)
XLA Modules:
  0.0 61.3 jit_solution(10510918828437140837)
XLA Ops:
  0.6 0.0 copy-start
  0.6 1.3 %copy-done = bf16[1,256,2560]{2,1,0:T(8,128)(2,1)S(1)} copy-done((bf16[1,256,2560]{2,1,0:T(8,128)(2,1)S(1)}, bf16[1,256,2560]{2,1,0:T(8,128)(2,1)}, u32[]{:S(2)}) %copy-start) | copy-done | bytes 1310744
  2.0 0.0 copy-start.1
  2.0 0.9 %copy-done.1 = bf16[1,256,512]{2,1,0:T(8,128)(2,1)S(1)} copy-done((bf16[1,256,512]{2,1,0:T(8,128)(2,1)S(1)}, bf16[1,256,512]{2,1,0:T(8,128)(2,1)}, u32[]{:S(2)}) %copy-start.1) | copy-done | bytes 262168
  2.9 0.0 copy-start.2
  2.9 0.9 %copy-done.2 = bf16[1,256,512]{2,1,0:T(8,128)(2,1)S(1)} copy-done((bf16[1,256,512]{2,1,0:T(8,128)(2,1)S(1)}, bf16[1,256,512]{2,1,0:T(8,128)(2,1)}, u32[]{:S(2)}) %copy-start.2) | copy-done | bytes 262168
  3.9 0.0 copy-start.3
  3.9 0.7 %copy-done.3 = s32[1,256]{1,0:T(1,128)S(1)} copy-done((s32[1,256]{1,0:T(1,128)S(1)}, s32[1,256]{1,0:T(1,128)}, u32[]{:S(2)}) %copy-start.3) | copy-done | bytes 1048
  4.5 53.7 %shard_map.76 = (bf16[256,2560]{1,0:T(8,128)(2,1)S(1)}, bf16[256,2560]{1,0:T(8,128)(2,1)S(1)}, bf16[2,256,512]{2,1,0:T(8,128)(2,1)S(1)}) custom-call(s32[1,256]{1,0:T(1,128)S(1)} %copy-done.3, bf16[256,2560]{1,0:T(8,128)(2,1)S(1)} %bitcast.9, bf16[256,512]{1,0:T(8,128)(2,1)S(1)} %bitcast.11, bf16[256,512]{1,0:T(8,128)(2,1)S(1)} %bitcast.12, ...), custom_call_target="tpu_custom_call" | custom-call | tf_op jit(solution)/shard_map/pallas_call | solution.py:285
  58.3 0.8 %select_bitcast_fusion.1 = bf16[1,2,256,512]{3,2,1,0:T(8,128)(2,1)} fusion(bf16[2,256,512]{2,1,0:T(8,128)(2,1)S(1)} %get-tuple-element.8, pred[]{:T(512)S(6)} %eq.3), kind=kLoop, calls=%fused_computation.1 | loop fusion | flops 262144 | bytes 1048577 | tf_op jit(solution)/shard_map/broadcast_in_dim | solution.py:323
  59.1 1.1 %select_bitcast_fusion = bf16[1,256,2560]{2,1,0:T(8,128)(2,1)} fusion(bf16[256,2560]{1,0:T(8,128)(2,1)S(1)} %get-tuple-element.7, pred[]{:T(512)S(6)} %eq.3), kind=kLoop, calls=%fused_computation | loop fusion | flops 655360 | bytes 2621441 | tf_op jit(solution)/shard_map/broadcast_in_dim | solution.py:323
  60.2 1.1 %copy.9 = bf16[1,256,2560]{2,1,0:T(8,128)(2,1)} copy(bf16[1,256,2560]{2,1,0:T(8,128)(2,1)S(1)} %bitcast.10) | data formatting | bytes 2621440
Async XLA Ops:
  0.6 1.3 %copy-start = (bf16[1,256,2560]{2,1,0:T(8,128)(2,1)S(1)}, bf16[1,256,2560]{2,1,0:T(8,128)(2,1)}, u32[]{:S(2)}) copy-start(bf16[1,256,2560]{2,1,0:T(8,128)(2,1)} %param.5) | copy-start | bytes 3932164
  2.0 0.9 %copy-start.1 = (bf16[1,256,512]{2,1,0:T(8,128)(2,1)S(1)}, bf16[1,256,512]{2,1,0:T(8,128)(2,1)}, u32[]{:S(2)}) copy-start(bf16[1,256,512]{2,1,0:T(8,128)(2,1)} %param.6) | copy-start | bytes 786436
  2.9 0.9 %copy-start.2 = (bf16[1,256,512]{2,1,0:T(8,128)(2,1)S(1)}, bf16[1,256,512]{2,1,0:T(8,128)(2,1)}, u32[]{:S(2)}) copy-start(bf16[1,256,512]{2,1,0:T(8,128)(2,1)} %param.7) | copy-start | bytes 786436
  3.9 0.7 %copy-start.3 = (s32[1,256]{1,0:T(1,128)S(1)}, s32[1,256]{1,0:T(1,128)}, u32[]{:S(2)}) copy-start(s32[1,256]{1,0:T(1,128)} %doc_ref.1) | copy-start | bytes 3076

commit v2 on v1

--- a/solution.py
+++ b/solution.py
@@ -269,6 +269,39 @@
         return 0
 
     lax.fori_loop(0, groups, drain, 0)
+
+
+def settle(sections, attn_in, dq_in, kv_in, attn_out, dq_out, kv_out, zero, sems):
+    last = lax.axis_index("section") == sections - 1
+    first = pltpu.make_async_copy(attn_in, attn_out, sems.at[0])
+    first.start()
+    narrow = kv_in.shape[2]
+
+    @pl.when(last)
+    def _():
+        zero[...] = jnp.zeros_like(zero)
+        copies = [pltpu.make_async_copy(zero, dq_out, sems.at[1])]
+        for i in range(2):
+            copies.append(
+                pltpu.make_async_copy(zero.at[:, pl.ds(0, narrow)], kv_out.at[i], sems.at[2 + i])
+            )
+        for copy in copies:
+            copy.start()
+        for copy in copies:
+            copy.wait()
+
+    @pl.when(jnp.logical_not(last))
+    def _():
+        copies = [
+            pltpu.make_async_copy(dq_in, dq_out, sems.at[1]),
+            pltpu.make_async_copy(kv_in, kv_out, sems.at[2]),
+        ]
+        for copy in copies:
+            copy.start()
+        for copy in copies:
+            copy.wait()
+
+    first.wait()
 
 
 def solution(mesh):
@@ -317,9 +350,14 @@
                 collective_id=0, has_side_effects=True, vmem_limit_bytes=48 * 2**20
             ),
         )(doc_start, queries[0], keys[0], values[0], output_cotangent[0])
-        last = lax.axis_index("section") == sections - 1
-        dq = jnp.where(last, jnp.zeros_like(dq), dq)
-        kv = jnp.where(last, jnp.zeros_like(kv), kv)
+        attn, dq, kv = pl.pallas_call(
+            functools.partial(settle, sections),
+            out_shape=tuple(jax.ShapeDtypeStruct(x.shape, x.dtype) for x in (attn, dq, kv)),
+            in_specs=[anywhere] * 3,
+            out_specs=(anywhere,) * 3,
+            scratch_shapes=[pltpu.VMEM((tok, wide), bf), dma((4,))],
+            compiler_params=pltpu.CompilerParams(vmem_limit_bytes=8 * 2**20),
+        )(attn, dq, kv)
         return attn[None], dq[None], kv[None]
 
     rows = P("section", "ctx", None)

time: 61.5 us -> 60.1 us (0.977)
  other arithmetic: 1.98 us -> 0 us
  Pallas kernels: 53.7 us -> 55.4 us
  local copies, waits for them, and re-layouts: 4.94 us -> 3.89 us
    broadcast_in_dim x2 -> x0, other arithmetic: 1.98 us -> none  [local(): return (attn[None], dq[None], kv[None])]
    pallas_call x0 -> x1, Pallas kernels: none -> 1.7 us  [local(): pl.pallas_call(functools.partial(settle, sections), out_shape=tuple((jax....]
    unnamed x9 -> x8, local copies, waits for them, and re-layouts: 4.94 us -> 3.89 us
where the time goes in v2:
time: 60.1 us; the launch traced here: 59.9 us
  Pallas kernels  55.4 us (92%)
  local copies, waits for them, and re-layouts  3.89 us (6%)
  between operations  0.65 us (1%)
    pallas_call x1, Pallas kernels, local(): pl.pallas_call(functools.partial(body, n, sections, groups, per), out_sha...  53.7 us
    unnamed x8, local copies, waits for them, and re-layouts  3.89 us
    pallas_call x1, Pallas kernels, local(): pl.pallas_call(functools.partial(settle, sections), out_shape=tuple((jax....  1.7 us

profile of v2, /device:TPU:19, one launch (start us, length us, event | category | flops | bytes accessed | tf_op | source)
XLA Modules:
  0.0 59.9 jit_solution(15783532885903511225)
XLA Ops:
  0.6 0.0 copy-start
  0.6 1.3 %copy-done = bf16[1,256,2560]{2,1,0:T(8,128)(2,1)S(1)} copy-done((bf16[1,256,2560]{2,1,0:T(8,128)(2,1)S(1)}, bf16[1,256,2560]{2,1,0:T(8,128)(2,1)}, u32[]{:S(2)}) %copy-start) | copy-done | bytes 1310744
  1.9 0.0 copy-start.1
  2.0 0.9 %copy-done.1 = bf16[1,256,512]{2,1,0:T(8,128)(2,1)S(1)} copy-done((bf16[1,256,512]{2,1,0:T(8,128)(2,1)S(1)}, bf16[1,256,512]{2,1,0:T(8,128)(2,1)}, u32[]{:S(2)}) %copy-start.1) | copy-done | bytes 262168
  2.9 0.0 copy-start.2
  2.9 0.9 %copy-done.2 = bf16[1,256,512]{2,1,0:T(8,128)(2,1)S(1)} copy-done((bf16[1,256,512]{2,1,0:T(8,128)(2,1)S(1)}, bf16[1,256,512]{2,1,0:T(8,128)(2,1)}, u32[]{:S(2)}) %copy-start.2) | copy-done | bytes 262168
  3.9 0.0 copy-start.3
  3.9 0.7 %copy-done.3 = s32[1,256]{1,0:T(1,128)S(1)} copy-done((s32[1,256]{1,0:T(1,128)S(1)}, s32[1,256]{1,0:T(1,128)}, u32[]{:S(2)}) %copy-start.3) | copy-done | bytes 1048
  4.5 53.7 %shard_map.76 = (bf16[256,2560]{1,0:T(8,128)(2,1)S(1)}, bf16[256,2560]{1,0:T(8,128)(2,1)S(1)}, bf16[2,256,512]{2,1,0:T(8,128)(2,1)S(1)}) custom-call(s32[1,256]{1,0:T(1,128)S(1)} %copy-done.3, bf16[256,2560]{1,0:T(8,128)(2,1)S(1)} %bitcast.7, bf16[256,512]{1,0:T(8,128)(2,1)S(1)} %bitcast.8, bf16[256,512]{1,0:T(8,128)(2,1)S(1)} %bitcast.9, ...), custom_call_target="tpu_custom_call" | custom-call | tf_op jit(solution)/shard_map/pallas_call | solution.py:318
  58.2 1.7 %shard_map.77 = (bf16[256,2560]{1,0:T(8,128)(2,1)}, bf16[256,2560]{1,0:T(8,128)(2,1)}, bf16[2,256,512]{2,1,0:T(8,128)(2,1)}) custom-call(bf16[256,2560]{1,0:T(8,128)(2,1)S(1)} %get-tuple-element.9.attn_in, bf16[256,2560]{1,0:T(8,128)(2,1)S(1)} %get-tuple-element.10.dq_in, bf16[2,256,512]{2,1,0:T(8,128)(2,1)S(1)} %get-tuple-element.11.kv_in), custom_call_target="tpu_custom_call" | custom-call | tf_op jit(solution)/shard_map/pallas_call | solution.py:353
Async XLA Ops:
  0.6 1.3 %copy-start = (bf16[1,256,2560]{2,1,0:T(8,128)(2,1)S(1)}, bf16[1,256,2560]{2,1,0:T(8,128)(2,1)}, u32[]{:S(2)}) copy-start(bf16[1,256,2560]{2,1,0:T(8,128)(2,1)} %param.5) | copy-start | bytes 3932164
  1.9 0.9 %copy-start.1 = (bf16[1,256,512]{2,1,0:T(8,128)(2,1)S(1)}, bf16[1,256,512]{2,1,0:T(8,128)(2,1)}, u32[]{:S(2)}) copy-start(bf16[1,256,512]{2,1,0:T(8,128)(2,1)} %param.6) | copy-start | bytes 786436
  2.9 0.9 %copy-start.2 = (bf16[1,256,512]{2,1,0:T(8,128)(2,1)S(1)}, bf16[1,256,512]{2,1,0:T(8,128)(2,1)}, u32[]{:S(2)}) copy-start(bf16[1,256,512]{2,1,0:T(8,128)(2,1)} %param.7) | copy-start | bytes 786436
  3.9 0.7 %copy-start.3 = (s32[1,256]{1,0:T(1,128)S(1)}, s32[1,256]{1,0:T(1,128)}, u32[]{:S(2)}) copy-start(s32[1,256]{1,0:T(1,128)} %doc_ref.1) | copy-start | bytes 3076
